TPU v7x, 128 devices: a whole 4x4x4 slice. The times are simulated.
128 devices in a mesh: dev: 128 (over y, x, z, core).
Axes of the slice: x: 4, y: 4, z: 4, core: 2. Of those that a mesh axis runs over, the one named last changes fastest.
Arguments:
- conductivity: float32 [512, 3, 2048], P('dev'), may hold values from 0.05 to 1
- block_ids: int32 [1024, 16], P('dev'), may hold values from 0 to 511, as said below
- weights: int32 [1024, 8], P('dev'), may hold values from 1 to 7
- source: float32 [1024, 3, 8, 16, 128], P('dev'), may hold values from -6 to 6
- cotangent: float32 [1024, 3, 8, 16, 128], P('dev'), may hold values from -6 to 6
Outputs:
- fields: float32 [1024, 3, 8, 16, 128], P('dev')
- gradient: float32 [512, 3, 2048], P('dev')
Inputs may be any that keep to these rules, and one draw needn't show every extreme that they name: `block_ids`: the 128 entries of the meshes of one device (an aligned block of 8 rows) name blocks of all owners, each owner exactly once, the owner of a block being its id // 4.
All inputs are finite; a program needn't handle non-finite values.
Results may differ from a plain program's by a relative error of at most 0.00002.
Values sent between devices are 32-bit elements; how exact they have to be, the bound alone decides.
A program may use at most 128 MiB of HBM per device.

v0:
```python
import jax, jax.numpy as jnp
from jax import lax
from jax.experimental import pallas as pl
from jax.experimental.pallas import tpu as pltpu
from jax.sharding import PartitionSpec as P

MX, MY, MZ, STEPS = 8, 16, 128, 10
HALF = STEPS // 2


def sweep(src, dst, mag, decay, masks, x, visit):
    first, last = masks
    olds = [[s(c, x, 0) for c in range(3)] for s in src]
    befores = [None] * len(src)
    for y in range(MY):
        keep = [decay[c, x, y] for c in range(3)]
        for k in range(len(src)):
            ex, ey, ez = olds[k]
            exz = jnp.where(last, 0.0, pltpu.roll(ex, MZ - 1, 1))
            eyz = jnp.where(last, 0.0, pltpu.roll(ey, MZ - 1, 1))
            eyx, ezx = src[k](1, x + 1, y), src[k](2, x + 1, y)
            h = mag[k]
            if y + 1 < MY:
                nexts = [src[k](c, x, y + 1) for c in range(3)]
                gx = h[0, x + 1, y] + ((nexts[2] - eyz) + (ey - ez))
                gz = h[2, x + 1, y] + ((eyx - nexts[0]) + (ex - ey))
            else:
                nexts = None
                gx = h[0, x + 1, y] + ((ey - ez) - eyz)
                gz = h[2, x + 1, y] + (eyx + (ex - ey))
            gy = h[1, x + 1, y] + ((exz - ezx) + (ez - ex))
            h[0, x + 1, y] = gx
            h[1, x + 1, y] = gy
            h[2, x + 1, y] = gz
            gxz = jnp.where(first, 0.0, pltpu.roll(gx, 1, 1))
            gyz = jnp.where(first, 0.0, pltpu.roll(gy, 1, 1))
            gyx, gzx = h[1, x, y], h[2, x, y]
            if y > 0:
                bx, bz = befores[k]
                cx = (gz - gy) + (gyz - bz)
                cz = (gy - gx) + (bx - gyx)
            else:
                cx = (gz - gy) + gyz
                cz = (gy - gx) - gyx
            cy = (gx - gz) + (gzx - gxz)
            new = [keep[c] * olds[k][c] - 0.25 * v for c, v in enumerate((cx, cy, cz))]
            visit(k, y, olds[k], new)
            befores[k] = (gx, gz)
            olds[k] = nexts


def compute_kernel(entry, weight, near, source, cotangent, fields, slots, hist, mag, decay, grad):
    lane = lax.broadcasted_iota(jnp.int32, (8, MZ), 1)
    masks = (lane == 0, lane == MZ - 1)
    zero = jnp.zeros((MY, 8, MZ), jnp.float32)
    for k in range(2):
        for c in range(3):
            mag[k, c, 0] = zero
            for n in range(HALF + 1):
                hist[k, n, c, MX] = zero

            def clear(x, carry):
                mag[k, c, x + 1] = zero
                return carry
            lax.fori_loop(0, MX, clear, 0)

    def stage(i, carry):
        c, x = i // MX, i % MX
        for y in range(MY):
            row = pl.ds(i * MY + y, 8, stride=3 * MX * MY)
            hist[0, 0, c, x, y] = source[row, :]
            hist[1, 0, c, x, y] = cotangent[row, :]
        return carry
    lax.fori_loop(0, 3 * MX, stage, 0)

    flat_decay = decay.reshape(3 * MX * MY * 8, MZ)
    flat_grad = grad.reshape(3 * MX * MY * 8, MZ)

    def blend(i, carry):
        m, x = i // MX, i % MX
        f = weight[m, x].astype(jnp.float32) * 0.125
        for c in range(3):
            close = near[c, entry[c, m * 2 * MX + x]]
            far = near[c, entry[c, m * 2 * MX + MX + x]]
            flat_decay[pl.ds((c * MX + x) * (MY * 8) + m, MY, stride=8), :] = 1.0 - 0.5 * (f * close + (1.0 - f) * far)
        return carry
    lax.fori_loop(0, 8 * MX, blend, 0)

    def early(n, carry):
        def plane(x, carry):
            src = [lambda c, xx, y, k=k: hist[k, n, c, xx, y] for k in range(2)]

            def visit(k, y, old, new):
                for c in range(3):
                    hist[k, n + 1, c, x, y] = new[c]
            sweep(src, None, [mag.at[0], mag.at[1]], decay, masks, x, visit)
            return carry
        return lax.fori_loop(0, MX, plane, carry)
    lax.fori_loop(0, HALF, early, 0)

    def late(n, carry):
        def plane(x, carry):
            src = [lambda c, xx, y, k=k: hist[k, HALF, c, xx, y] for k in range(2)]
            part = {}

            def visit(k, y, old, new):
                terms = [old[c] * hist[1 - k, STEPS - 1 - n, c, x, y] for c in range(3)]
                if k == 0:
                    part[y] = terms
                else:
                    for c in range(3):
                        grad[c, x, y] = (grad[c, x, y] if n is not HALF else 0.0) + (part[y][c] + terms[c])
                for c in range(3):
                    hist[k, HALF, c, x, y] = new[c]
            sweep(src, None, [mag.at[0], mag.at[1]], decay, masks, x, visit)
            return carry
        return lax.fori_loop(0, MX, plane, carry)
    late(HALF, 0)
    lax.fori_loop(HALF + 1, STEPS - 1, late, 0)

    def final(x, carry):
        src = [lambda c, xx, y: hist[0, HALF, c, xx, y]]

        def visit(k, y, old, new):
            for c in range(3):
                fields[pl.ds((c * MX + x) * MY + y, 8, stride=3 * MX * MY), :] = new[c]
                grad[c, x, y] = grad[c, x, y] + (old[c] * hist[1, 0, c, x, y] + hist[1, HALF, c, x, y] * hist[0, 0, c, x, y])
        sweep(src, None, [mag.at[0]], decay, masks, x, visit)
        return carry
    lax.fori_loop(0, MX, final, 0)

    def spread(i, carry):
        m, x = i // MX, i % MX
        f = weight[m, x].astype(jnp.float32) * 0.125
        for c in range(3):
            g = flat_grad[pl.ds((c * MX + x) * (MY * 8) + m, MY, stride=8), :]
            slots[c, entry[c, m * 2 * MX + x]] = (-0.5 * f) * g
            slots[c, entry[c, m * 2 * MX + MX + x]] = (-0.5 * (1.0 - f)) * g
        return carry
    lax.fori_loop(0, 8 * MX, spread, 0)


def compute(entry, weight, near, source, cotangent):
    vmem = pl.BlockSpec(memory_space=pltpu.VMEM)
    smem = pl.BlockSpec(memory_space=pltpu.SMEM)
    f32 = jnp.float32
    return pl.pallas_call(
        compute_kernel,
        out_shape=(jax.ShapeDtypeStruct((8 * 3 * MX * MY, MZ), f32), jax.ShapeDtypeStruct((3, 128, MY, MZ), f32)),
        in_specs=[smem, smem, vmem, vmem, vmem],
        out_specs=(vmem, vmem),
        scratch_shapes=[
            pltpu.VMEM((2, HALF + 1, 3, MX + 1, MY, 8, MZ), f32),
            pltpu.VMEM((2, 3, MX + 1, MY, 8, MZ), f32),
            pltpu.VMEM((3, MX, MY, 8, MZ), f32),
            pltpu.VMEM((3, MX, MY, 8, MZ), f32),
        ],
        compiler_params=pltpu.CompilerParams(vmem_limit_bytes=60 * 2**20),
    )(entry, weight, near, source, cotangent)


def local(conductivity, block_ids, weights, source, cotangent):
    count = lax.axis_size("dev")
    blocks_here = conductivity.shape[0]
    flat = block_ids.reshape(-1)
    owner, index = flat // blocks_here, flat % blocks_here
    hit = owner[:, None] == jnp.arange(count, dtype=jnp.int32)[None, :]
    wanted = jnp.sum(jnp.where(hit, index[:, None], 0), axis=0).astype(jnp.int32)
    asked = lax.all_to_all(wanted.reshape(count, 1), "dev", split_axis=0, concat_axis=0, tiled=True).reshape(count)
    blocks = conductivity.reshape(blocks_here, 3, MY, MZ)
    pick = asked[:, None, None, None]
    outgoing = jnp.where(
        pick < 2, jnp.where(pick == 0, blocks[:1], blocks[1:2]), jnp.where(pick == 2, blocks[2:3], blocks[3:])
    )
    arrived = lax.all_to_all(outgoing, "dev", split_axis=0, concat_axis=0, tiled=True)
    fields, slots = compute(
        jnp.stack([owner] * 3), weights, arrived.transpose(1, 0, 2, 3), source.reshape(-1, MZ), cotangent.reshape(-1, MZ)
    )
    back = lax.all_to_all(slots.transpose(1, 0, 2, 3), "dev", split_axis=0, concat_axis=0, tiled=True)
    gradient = jnp.stack(
        [jnp.sum(jnp.where((asked == k)[:, None, None, None], back, 0.0), axis=0) for k in range(4)]
    )
    return fields.reshape(source.shape), gradient.reshape(conductivity.shape)


def solution(mesh):
    rows = P("dev")
    return jax.shard_map(
        local, mesh=mesh, in_specs=(rows,) * 5, out_specs=(rows, rows), check_vma=False
    )
```

profile of v0, /device:TPU:1, one launch (start us, length us, event | category | flops | bytes accessed | tf_op | source)
XLA Modules:
  0.0 167.9 jit_solution(2551142144577201253)
XLA Ops:
  0.6 0.8 reshape.141
  1.4 0.1 select_reduce_fusion.4
  1.5 0.7 copy.13
  2.3 11.5 %all-to-all-start = ((s32[128,1,1]{2,1,0:T(1,128)}), s32[128,1,1]{2,1,0:T(1,128)S(1)}, u32[]{:S(2)}, u32[]{:S(2)}) async-start(s32[128,1,1]{2,1,0:T(1,128)} %copy.13), calls=%async_computation | async-start | bytes 131072 | tf_op jit(solution)/shard_map/all_to_all | solution.py:169
  13.8 1.2 fusion
  15.0 8.1 %all-to-all-done = s32[128,1,1]{2,1,0:T(1,128)S(1)} async-done(((s32[128,1,1]{2,1,0:T(1,128)}), s32[128,1,1]{2,1,0:T(1,128)S(1)}, u32[]{:S(2)}, u32[]{:S(2)}) %all-to-all-start) | async-done | bytes 544 | tf_op jit(solution)/shard_map/all_to_all | solution.py:169
  23.1 11.4 %compare_reduce_fusion.1 = (pred[128]{0:T(512)(128)(4,1)S(1)}, pred[128]{0:T(512)(128)(4,1)S(1)}, pred[128]{0:T(512)(128)(4,1)S(1)}, pred[128]{0:T(512)(128)(4,1)S(1)}, pred[128]{0:T(512)(128)(4,1)S(1)}) fusion(s32[128,1,1]{2,1,0:T(1,128)S(1)} %all-to-all-done), kind=kLoop, calls=%fused_computation.7 | loop fusion | flops 640 | bytes 1152 | tf_op jit(solution)/shard_map/eq | solution.py:181
  34.5 0.5 select_select_fusion
  35.0 45.8 %all_to_all.19 = f32[128,3,16,128]{3,2,1,0:T(8,128)S(1)} all-to-all(f32[128,3,16,128]{3,2,1,0:T(8,128)S(1)} %select_select_fusion), channel_id=1, replica_groups=mesh['dev'=128] {'dev'}, dimensions={0} | all-to-all | bytes 6291456 | tf_op jit(solution)/shard_map/all_to_all | solution.py:175
  80.9 2.0 %copy.17 = f32[128,3,16,128]{3,2,0,1:T(8,128)} copy(f32[128,3,16,128]{3,2,1,0:T(8,128)S(1)} %all_to_all.19) | data formatting | bytes 6291456 | tf_op jit(solution)/shard_map/all_to_all | solution.py:175
  82.8 0.6 stack.21.entry
  83.4 34.6 %shard_map.68 = (f32[3072,128]{1,0:T(8,128)}, f32[3,128,16,128]{3,2,1,0:T(8,128)}) custom-call(s32[3,128]{1,0:T(4,128)} %stack.21.entry, s32[8,8]{1,0:T(8,128)} %weight.1, f32[3,128,16,128]{3,2,1,0:T(8,128)} %bitcast.16, f32[3072,128]{1,0:T(8,128)} %bitcast.18, f32[3072,128]{1,0:T(8,128)} %bitcast.19), custom_call_target="tpu_custom_call" | custom-call | tf_op jit(solution)/shard_map/pallas_call | solution.py:147
  118.0 2.1 %copy.15 = f32[128,3,16,128]{3,2,1,0:T(8,128)S(1)} copy(f32[128,3,16,128]{3,2,0,1:T(8,128)} %bitcast.17) | data formatting | bytes 6291456 | tf_op jit(solution)/shard_map/transpose | solution.py:179
  120.1 45.7 %all_to_all.20 = f32[128,3,16,128]{3,2,1,0:T(8,128)S(1)} all-to-all(f32[128,3,16,128]{3,2,1,0:T(8,128)S(1)} %copy.15), channel_id=1, replica_groups=mesh['dev'=128] {'dev'}, dimensions={0} | all-to-all | bytes 6291456 | tf_op jit(solution)/shard_map/all_to_all | solution.py:179
  165.8 1.3 select_reduce_fusion.3
  167.1 0.7 pad_maximum_fusion
  (1 shorter events, 0.0 us)
Async XLA Ops:
  2.3 20.8 %all-to-all-start = ((s32[128,1,1]{2,1,0:T(1,128)}), s32[128,1,1]{2,1,0:T(1,128)S(1)}, u32[]{:S(2)}, u32[]{:S(2)}) async-start(s32[128,1,1]{2,1,0:T(1,128)} %copy.13), calls=%async_computation | async-start | bytes 131072 | tf_op jit(solution)/shard_map/all_to_all | solution.py:169
where the time goes:
time: 168 us
  blocking collectives  91.5 us (54%)
  Pallas kernels  34.6 us (21%)
  other arithmetic  14.1 us (8%)
  starting transfers between devices  11.5 us (7%)
  waiting for transfers between devices  8.15 us (5%)
  local copies, waits for them, and re-layouts  7.32 us (4%)
    all_to_all x1, blocking collectives, local(): lax.all_to_all(outgoing, 'dev', split_axis=0, concat_axis=0, tiled=True)  45.8 us
    all_to_all x1, blocking collectives, local(): lax.all_to_all(slots.transpose(1, 0, 2, 3), 'dev', split_axis=0, concat_a...  45.7 us
    pallas_call x1, Pallas kernels, compute(): pl.pallas_call(compute_kernel, out_shape=(jax.ShapeDtypeStruct((8 * 3 * M...  34.6 us
    all_to_all x1, starting transfers between devices, local(): lax.all_to_all(wanted.reshape(count, 1), 'dev', split_axis=0, concat_axis...  11.5 us
    eq x1, other arithmetic, local(): asked == k  11.4 us
    all_to_all x1, waiting for transfers between devices, local(): lax.all_to_all(wanted.reshape(count, 1), 'dev', split_axis=0, concat_axis...  8.15 us
  transfers between devices with their start and end apart: 1, of which 1 were waited for; matrix products, arithmetic and copies ran while one was open for 1% of the time, Pallas kernels for 0%

commit v1 on v0

--- a/solution.py
+++ b/solution.py
@@ -6,6 +6,242 @@
 
 MX, MY, MZ, STEPS = 8, 16, 128, 10
 HALF = STEPS // 2
+MESH = pl.DeviceIdType.MESH
+STRIDE = {"y": 32, "x": 8, "z": 2}
+ORDERS = (("y", "x", "z"), ("x", "z", "y"), ("z", "y", "x"))
+FAR = (2, 1, 3)
+
+
+def place():
+    me = lax.axis_index("dev")
+    return me, {"y": me // 32, "x": (me // 8) % 4, "z": (me // 2) % 4}, me % 2
+
+
+def shifted(me, at, dim, k):
+    return me + ((at[dim] + k) % 4 - at[dim]) * STRIDE[dim]
+
+
+def other_core(me, core, q):
+    return me + (1 - 2 * core) * q
+
+
+def column(me, at, core, dim, t, q):
+    return other_core(shifted(me, at, dim, t), core, q)
+
+
+def neighbours(me, at, core):
+    out = [other_core(me, core, 1)]
+    for dim in ("y", "x", "z"):
+        for t in FAR:
+            for q in (0, 1):
+                out.append(column(me, at, core, dim, t, q))
+    return out
+
+
+def greet(me, at, core):
+    barrier = pltpu.get_barrier_semaphore()
+    near = neighbours(me, at, core)
+    for other in near:
+        pl.semaphore_signal(barrier, inc=1, device_id=(other,), device_id_type=MESH)
+    pl.semaphore_wait(barrier, len(near))
+
+
+def remote(src, dst, send, recv, device):
+    return pltpu.make_async_remote_copy(
+        src_ref=src, dst_ref=dst, send_sem=send, recv_sem=recv, device_id=(device,), device_id_type=MESH
+    )
+
+
+DIMS = ("y", "x", "z")
+REACH = [(t, q) for t in (2, 1, 3, 0) for q in (1, 0) if (t, q) != (0, 0)]
+
+
+def fetch_kernel(ids, model, arrived, asked, wish, gather, picked, asked_s, asked_v,
+                 s_wish, r_wish, s_a1, r_a1, s_a2, r_a2, s_b, r_b, s_loc):
+    me, at, core = place()
+    pair = other_core(me, core, 1)
+    lane = lax.broadcasted_iota(jnp.int32, (8, MZ), 1)
+
+    def request(e, wanted):
+        block = ids[e // 16, e % 16]
+        return jnp.where(lane == (block >> 2), block & 3, wanted)
+    wanted = lax.fori_loop(0, 128, request, jnp.zeros((8, MZ), jnp.int32))
+    wish[...] = wanted
+    for c, (a1, a2, b) in enumerate(ORDERS):
+        asked_v[c, 0, 0] = wanted
+        for k in range(4):
+            gather[c][0][at[a1], k] = model[pl.ds(c * 64 + k, MY, stride=4), :]
+    greet(me, at, core)
+    started = []
+
+    def go(copy):
+        copy.start()
+        started.append(copy)
+
+    for k in FAR:
+        for c, (a1, a2, b) in enumerate(ORDERS):
+            own = gather[c][0].at[at[a1]]
+            go(remote(own, own, s_a1.at[c, k], r_a1.at[c, k], shifted(me, at, a1, k)))
+    for c, (a1, a2, b) in enumerate(ORDERS):
+        for t, q in REACH:
+            go(remote(wish, asked_v.at[c, t, q], s_wish.at[c, t, q], r_wish.at[c, t, q], column(me, at, core, b, t, q)))
+    for j in (0, 1, 3, 2):
+        for c, (a1, a2, b) in enumerate(ORDERS):
+            at_j = (at[a1] + 4 - j) % 4
+            slot = gather[c][0].at[at_j]
+            if j:
+                remote(slot, slot, s_a1.at[c, j], r_a1.at[c, j], pair).wait_recv()
+            for k in FAR:
+                go(remote(slot, gather[c][k].at[at_j], s_a2.at[c, k, j], r_a2.at[c, k, j], shifted(me, at, a2, k)))
+    for c in range(3):
+        for t, q in REACH:
+            remote(wish, asked_v.at[c, t, q], s_wish.at[c, t, q], r_wish.at[c, t, q], pair).wait_recv()
+    loc = pltpu.make_async_copy(asked_v, asked_s, s_loc)
+    loc.start()
+    loc.wait()
+    for k in (0, 1, 3, 2):
+        for c, (a1, a2, b) in enumerate(ORDERS):
+            row = (at[a2] + 4 - k) % 4
+            if k:
+                for j in range(4):
+                    slot = gather[c][k].at[(at[a1] + 4 - j) % 4]
+                    remote(slot, slot, s_a2.at[c, k, j], r_a2.at[c, k, j], pair).wait_recv()
+            base = me + (row - at[a2]) * STRIDE[a2] - at[a1] * STRIDE[a1]
+            for t, q in REACH + [(0, 0)]:
+                for i in range(4):
+                    block = gather[c][k][i, asked_s[c, (4 - t) % 4, q, 0, base + i * STRIDE[a1]]]
+                    if (t, q) == (0, 0):
+                        arrived[c, at[b], core, row, i] = block
+                    else:
+                        picked[c, t, q, row, i] = block
+                if (t, q) != (0, 0):
+                    go(remote(picked.at[c, t, q, row], arrived.at[c, at[b], core, row],
+                              s_b.at[c, k, t, q], r_b.at[c, k, t, q], column(me, at, core, b, t, q)))
+    asked[...] = asked_v[...]
+    for k in range(4):
+        for c, (a1, a2, b) in enumerate(ORDERS):
+            row = (at[a2] + 4 - k) % 4
+            for t, q in REACH:
+                slot = arrived.at[c, (at[b] + 4 - t) % 4, core + (1 - 2 * core) * q, row]
+                remote(slot, slot, s_b.at[c, k, t, q], r_b.at[c, k, t, q], pair).wait_recv()
+    for copy in started:
+        copy.wait_send()
+
+
+def fetch(ids, model):
+    vmem = pl.BlockSpec(memory_space=pltpu.VMEM)
+    smem = pl.BlockSpec(memory_space=pltpu.SMEM)
+    f32, i32 = jnp.float32, jnp.int32
+    dma = pltpu.SemaphoreType.DMA
+    return pl.pallas_call(
+        fetch_kernel,
+        out_shape=(jax.ShapeDtypeStruct((3, 4, 2, 4, 4, MY, MZ), f32), jax.ShapeDtypeStruct((3, 4, 2, 8, MZ), i32)),
+        in_specs=[smem, vmem],
+        out_specs=(vmem, vmem),
+        scratch_shapes=[
+            pltpu.VMEM((8, MZ), i32),
+            [[pltpu.VMEM((4, 4, MY, MZ), f32) for k in range(4)] for c in range(3)],
+            pltpu.VMEM((3, 4, 2, 4, 4, MY, MZ), f32),
+            pltpu.SMEM((3, 4, 2, 8, MZ), i32),
+            pltpu.VMEM((3, 4, 2, 8, MZ), i32),
+            dma((3, 4, 2)), dma((3, 4, 2)),
+            dma((3, 4)), dma((3, 4)),
+            dma((3, 4, 4)), dma((3, 4, 4)),
+            dma((3, 4, 4, 2)), dma((3, 4, 4, 2)),
+            dma,
+        ],
+        compiler_params=pltpu.CompilerParams(collective_id=0, has_side_effects=True, vmem_limit_bytes=32 * 2**20),
+    )(ids, model)
+
+
+def give_kernel(asked, slots, gradient, landed, part, part_in, row_sum, row_in,
+                s_b, r_b, s_a2, r_a2, s_a1, r_a1):
+    me, at, core = place()
+    pair = other_core(me, core, 1)
+    greet(me, at, core)
+    started = []
+
+    def go(copy):
+        copy.start()
+        started.append(copy)
+
+    def landing(c, t, q, row, k, b, device):
+        return remote(slots.at[c, (at[b] + t) % 4, core + (1 - 2 * core) * q, row], landed.at[c, t, q, row],
+                      s_b.at[c, k, t, q], r_b.at[c, k, t, q], device)
+
+    def rowwise(c, k, j, i, a2):
+        return remote(part.at[c, k, i], part_in.at[c, k, i], s_a2.at[c, k, j], r_a2.at[c, k, j], shifted(me, at, a2, k))
+
+    for k in (2, 1, 3, 0):
+        for c, (a1, a2, b) in enumerate(ORDERS):
+            for t, q in REACH:
+                go(landing(c, t, q, (at[a2] + k) % 4, k, b, column(me, at, core, b, t, q)))
+    for k in (2, 1, 3, 0):
+        for c, (a1, a2, b) in enumerate(ORDERS):
+            row = (at[a2] + k) % 4
+            for t, q in REACH:
+                landing(c, t, q, row, k, b, pair).wait_recv()
+            base = me + (row - at[a2]) * STRIDE[a2] - at[a1] * STRIDE[a1]
+            for j in (2, 1, 3, 0):
+                i = (at[a1] + j) % 4
+                own = slots[c, at[b], core, row, i]
+                who = asked[c, 0, 0, 0, base + i * STRIDE[a1]]
+                total = [jnp.where(who == n, own, 0.0) for n in range(4)]
+                for t, q in REACH:
+                    term = landed[c, t, q, row, i]
+                    who = asked[c, t, q, 0, base + i * STRIDE[a1]]
+                    total = [v + jnp.where(who == n, term, 0.0) for n, v in enumerate(total)]
+                for n in range(4):
+                    part[c, k, i, n] = total[n]
+                if k:
+                    go(rowwise(c, k, j, i, a2))
+    for j in (2, 1, 3, 0):
+        for c, (a1, a2, b) in enumerate(ORDERS):
+            i = (at[a1] + j) % 4
+            for k in FAR:
+                rowwise(c, k, j, i, a2).wait_recv()
+            for n in range(4):
+                row_sum[c, j, n] = (part[c, 0, i, n] + part_in[c, 1, i, n]) + (part_in[c, 2, i, n] + part_in[c, 3, i, n])
+            if j:
+                go(remote(row_sum.at[c, j], row_in.at[c, j], s_a1.at[c, j], r_a1.at[c, j], shifted(me, at, a1, j)))
+    for c, (a1, a2, b) in enumerate(ORDERS):
+        for j in FAR:
+            remote(row_sum.at[c, j], row_in.at[c, j], s_a1.at[c, j], r_a1.at[c, j], pair).wait_recv()
+        for n in range(4):
+            gradient[pl.ds(c * 64 + n, MY, stride=4), :] = (row_sum[c, 0, n] + row_in[c, 1, n]) + (row_in[c, 2, n] + row_in[c, 3, n])
+    for copy in started:
+        copy.wait_send()
+
+
+def give(asked, slots):
+    vmem = pl.BlockSpec(memory_space=pltpu.VMEM)
+    smem = pl.BlockSpec(memory_space=pltpu.SMEM)
+    f32 = jnp.float32
+    dma = pltpu.SemaphoreType.DMA
+    return pl.pallas_call(
+        give_kernel,
+        out_shape=jax.ShapeDtypeStruct((192, MZ), f32),
+        in_specs=[smem, vmem],
+        out_specs=vmem,
+        scratch_shapes=[
+            pltpu.VMEM((3, 4, 2, 4, 4, MY, MZ), f32),
+            pltpu.VMEM((3, 4, 4, 4, MY, MZ), f32),
+            pltpu.VMEM((3, 4, 4, 4, MY, MZ), f32),
+            pltpu.VMEM((3, 4, 4, MY, MZ), f32),
+            pltpu.VMEM((3, 4, 4, MY, MZ), f32),
+            dma((3, 4, 4, 2)), dma((3, 4, 4, 2)),
+            dma((3, 4, 4)), dma((3, 4, 4)),
+            dma((3, 4)), dma((3, 4)),
+        ],
+        compiler_params=pltpu.CompilerParams(collective_id=1, has_side_effects=True, vmem_limit_bytes=32 * 2**20),
+    )(asked, slots)
+
+
+def spot(c, block):
+    o = block >> 2
+    to = {"y": o >> 5, "x": (o >> 3) & 3, "z": (o >> 1) & 3}
+    a1, a2, b = ORDERS[c]
+    return ((to[b] * 2 + (o & 1)) * 4 + to[a2]) * 4 + to[a1]
 
 
 def sweep(src, dst, mag, decay, masks, x, visit):
@@ -80,8 +316,8 @@
         m, x = i // MX, i % MX
         f = weight[m, x].astype(jnp.float32) * 0.125
         for c in range(3):
-            close = near[c, entry[c, m * 2 * MX + x]]
-            far = near[c, entry[c, m * 2 * MX + MX + x]]
+            close = near[c, spot(c, entry[m, x])]
+            far = near[c, spot(c, entry[m, MX + x])]
             flat_decay[pl.ds((c * MX + x) * (MY * 8) + m, MY, stride=8), :] = 1.0 - 0.5 * (f * close + (1.0 - f) * far)
         return carry
     lax.fori_loop(0, 8 * MX, blend, 0)
@@ -134,8 +370,8 @@
         f = weight[m, x].astype(jnp.float32) * 0.125
         for c in range(3):
             g = flat_grad[pl.ds((c * MX + x) * (MY * 8) + m, MY, stride=8), :]
-            slots[c, entry[c, m * 2 * MX + x]] = (-0.5 * f) * g
-            slots[c, entry[c, m * 2 * MX + MX + x]] = (-0.5 * (1.0 - f)) * g
+            slots[c, spot(c, entry[m, x])] = (-0.5 * f) * g
+            slots[c, spot(c, entry[m, MX + x])] = (-0.5 * (1.0 - f)) * g
         return carry
     lax.fori_loop(0, 8 * MX, spread, 0)
 
@@ -160,26 +396,14 @@
 
 
 def local(conductivity, block_ids, weights, source, cotangent):
-    count = lax.axis_size("dev")
-    blocks_here = conductivity.shape[0]
-    flat = block_ids.reshape(-1)
-    owner, index = flat // blocks_here, flat % blocks_here
-    hit = owner[:, None] == jnp.arange(count, dtype=jnp.int32)[None, :]
-    wanted = jnp.sum(jnp.where(hit, index[:, None], 0), axis=0).astype(jnp.int32)
-    asked = lax.all_to_all(wanted.reshape(count, 1), "dev", split_axis=0, concat_axis=0, tiled=True).reshape(count)
-    blocks = conductivity.reshape(blocks_here, 3, MY, MZ)
-    pick = asked[:, None, None, None]
-    outgoing = jnp.where(
-        pick < 2, jnp.where(pick == 0, blocks[:1], blocks[1:2]), jnp.where(pick == 2, blocks[2:3], blocks[3:])
+    blocks = conductivity.shape[0]
+    model = conductivity.reshape(blocks, 3, MY, MZ).transpose(1, 2, 0, 3).reshape(3 * MY * blocks, MZ)
+    arrived, asked = fetch(block_ids, model)
+    fields, slots = compute(
+        block_ids, weights, arrived.reshape(3, 128, MY, MZ), source.reshape(-1, MZ), cotangent.reshape(-1, MZ)
     )
-    arrived = lax.all_to_all(outgoing, "dev", split_axis=0, concat_axis=0, tiled=True)
-    fields, slots = compute(
-        jnp.stack([owner] * 3), weights, arrived.transpose(1, 0, 2, 3), source.reshape(-1, MZ), cotangent.reshape(-1, MZ)
-    )
-    back = lax.all_to_all(slots.transpose(1, 0, 2, 3), "dev", split_axis=0, concat_axis=0, tiled=True)
-    gradient = jnp.stack(
-        [jnp.sum(jnp.where((asked == k)[:, None, None, None], back, 0.0), axis=0) for k in range(4)]
-    )
+    gradient = give(asked, slots.reshape(arrived.shape))
+    gradient = gradient.reshape(3, MY, blocks, MZ).transpose(2, 0, 1, 3)
     return fields.reshape(source.shape), gradient.reshape(conductivity.shape)
 
 

time: 168 us -> 107 us (0.64)
  blocking collectives: 91.5 us -> 0 us
  Pallas kernels: 34.6 us -> 101 us
  other arithmetic: 14.1 us -> 0 us
  starting transfers between devices: 11.5 us -> 0 us
  waiting for transfers between devices: 8.15 us -> 0 us
    all_to_all x2 -> x0, blocking collectives: 91.5 us -> none  [the longest x1 45.8 us: local(): lax.all_to_all(outgoing, 'dev', split_axis=0, concat_axis=0, tiled=True)]
    pallas_call x0 -> x2, Pallas kernels: none -> 63.3 us  [the longest x1 35.3 us: fetch(): pl.pallas_call(fetch_kernel, out_shape=(jax.ShapeDtypeStruct((3, 4, 2, 4,...]
    all_to_all x1 -> x0, starting transfers between devices: 11.5 us -> none  [local(): lax.all_to_all(wanted.reshape(count, 1), 'dev', split_axis=0, concat_axis...]
    eq x1 -> x0, other arithmetic: 11.4 us -> none  [local(): asked == k]
    all_to_all x1 -> x0, waiting for transfers between devices: 8.15 us -> none  [local(): lax.all_to_all(wanted.reshape(count, 1), 'dev', split_axis=0, concat_axis...]
    unnamed x0 -> x9, local copies, waits for them, and re-layouts: none -> 5.75 us
    all_to_all x2 -> x0, local copies, waits for them, and re-layouts: 2.71 us -> none  [the longest x1 1.96 us: local(): lax.all_to_all(outgoing, 'dev', split_axis=0, concat_axis=0, tiled=True)]
    pallas_call x1, Pallas kernels: 34.6 us -> 37.2 us  [compute(): pl.pallas_call(compute_kernel, out_shape=(jax.ShapeDtypeStruct((8 * 3 * M...]
  transfers between devices with their start and end apart: 1 -> 0, of which waited for: 1 -> 0; matrix products, arithmetic and copies ran while one was open for 1% -> 0% of each run, Pallas kernels for 0% -> 0%
where the time goes in v1:
time: 107 us
  Pallas kernels  101 us (94%)
  local copies, waits for them, and re-layouts  5.75 us (5%)
    pallas_call x1, Pallas kernels, compute(): pl.pallas_call(compute_kernel, out_shape=(jax.ShapeDtypeStruct((8 * 3 * M...  37.2 us
    pallas_call x1, Pallas kernels, fetch(): pl.pallas_call(fetch_kernel, out_shape=(jax.ShapeDtypeStruct((3, 4, 2, 4,...  35.3 us
    pallas_call x1, Pallas kernels, give(): pl.pallas_call(give_kernel, out_shape=jax.ShapeDtypeStruct((192, MZ), f32...  28 us
    unnamed x9, local copies, waits for them, and re-layouts  5.75 us

profile of v1, /device:TPU:1, one launch (start us, length us, event | category | flops | bytes accessed | tf_op | source)
XLA Modules:
  0.0 107.0 jit_solution(9206862285804131959)
XLA Ops:
  0.6 0.0 copy-start.2
  0.6 0.9 copy-done.2
  1.5 0.0 copy-start.3
  1.5 0.7 copy-done.3
  2.2 35.3 %shard_map.68 = (f32[3,4,2,4,4,16,128]{6,5,4,3,2,1,0:T(8,128)S(1)}, s32[3,4,2,8,128]{4,3,2,1,0:T(8,128)S(1)}) custom-call(s32[8,16]{1,0:T(8,128)S(1)} %copy-done.3, f32[192,128]{1,0:T(8,128)S(1)} %bitcast.18), custom_call_target="tpu_custom_call" | custom-call | tf_op jit(solution)/shard_map/pallas_call | solution.py:136
  37.5 0.0 copy-start
  37.5 1.6 %copy-done = f32[3,4,2,4,4,16,128]{6,5,4,3,2,1,0:T(8,128)} copy-done((f32[3,4,2,4,4,16,128]{6,5,4,3,2,1,0:T(8,128)}, f32[3,4,2,4,4,16,128]{6,5,4,3,2,1,0:T(8,128)S(1)}, u32[]{:S(2)}) %copy-start) | copy-done | bytes 3145752
  39.2 37.2 %shard_map.69 = (f32[3072,128]{1,0:T(8,128)}, f32[3,128,16,128]{3,2,1,0:T(8,128)}) custom-call(s32[8,16]{1,0:T(8,128)} %entry.1, s32[8,8]{1,0:T(8,128)} %weight.1, f32[3,128,16,128]{3,2,1,0:T(8,128)} %bitcast.15, f32[3072,128]{1,0:T(8,128)} %bitcast.19, f32[3072,128]{1,0:T(8,128)} %bitcast.20), custom_call_target="tpu_custom_call" | custom-call | tf_op jit(solution)/shard_map/pallas_call | solution.py:383
  76.4 0.0 copy-start.1
  76.4 1.9 %copy-done.1 = f32[3,128,16,128]{3,2,1,0:T(8,128)S(1)} copy-done((f32[3,128,16,128]{3,2,1,0:T(8,128)S(1)}, f32[3,128,16,128]{3,2,1,0:T(8,128)}, u32[]{:S(2)}) %copy-start.1) | copy-done | bytes 3145752
  78.3 28.0 %shard_map.70 = f32[192,128]{1,0:T(8,128)S(1)} custom-call(s32[3,4,2,8,128]{4,3,2,1,0:T(8,128)S(1)} %get-tuple-element.8.asked, f32[3,4,2,4,4,16,128]{6,5,4,3,2,1,0:T(8,128)S(1)} %bitcast.16), custom_call_target="tpu_custom_call" | custom-call | tf_op jit(solution)/shard_map/pallas_call | solution.py:221
  106.4 0.6 copy.10
Async XLA Ops:
  0.6 0.9 copy-start.2
  1.5 0.7 copy-start.3
  37.5 1.7 %copy-start = (f32[3,4,2,4,4,16,128]{6,5,4,3,2,1,0:T(8,128)}, f32[3,4,2,4,4,16,128]{6,5,4,3,2,1,0:T(8,128)S(1)}, u32[]{:S(2)}) copy-start(f32[3,4,2,4,4,16,128]{6,5,4,3,2,1,0:T(8,128)S(1)} %get-tuple-element.6) | copy-start | bytes 9437188
  76.4 1.9 %copy-start.1 = (f32[3,128,16,128]{3,2,1,0:T(8,128)S(1)}, f32[3,128,16,128]{3,2,1,0:T(8,128)}, u32[]{:S(2)}) copy-start(f32[3,128,16,128]{3,2,1,0:T(8,128)} %get-tuple-element.9) | copy-start | bytes 9437188

commit v2 on v0

v2 whole, which is shorter than its diff:
```python
import jax, jax.numpy as jnp
from jax import lax
from jax.experimental import pallas as pl
from jax.experimental.pallas import tpu as pltpu
from jax.sharding import PartitionSpec as P

MX, MY, MZ, STEPS = 8, 16, 128, 10
HALF = STEPS // 2
MESH = pl.DeviceIdType.MESH
STRIDE = {"y": 32, "x": 8, "z": 2}
ORDERS = (("y", "x", "z"), ("x", "z", "y"), ("z", "y", "x"))
FAR = (2, 1, 3)


def place():
    me = lax.axis_index("dev")
    return me, {"y": me // 32, "x": (me // 8) % 4, "z": (me // 2) % 4}, me % 2


def shifted(me, at, dim, k):
    return me + ((at[dim] + k) % 4 - at[dim]) * STRIDE[dim]


def other_core(me, core, q):
    return me + (1 - 2 * core) * q


def column(me, at, core, dim, t, q):
    return other_core(shifted(me, at, dim, t), core, q)


def neighbours(me, at, core):
    out = [other_core(me, core, 1)]
    for dim in ("y", "x", "z"):
        for t in FAR:
            for q in (0, 1):
                out.append(column(me, at, core, dim, t, q))
    return out


def remote(src, dst, send, recv, device):
    return pltpu.make_async_remote_copy(
        src_ref=src, dst_ref=dst, send_sem=send, recv_sem=recv, device_id=(device,), device_id_type=MESH
    )


REACH = [(t, q) for t in (2, 1, 3, 0) for q in (1, 0) if (t, q) != (0, 0)]


def spot(c, block):
    o = block >> 2
    to = {"y": o >> 5, "x": (o >> 3) & 3, "z": (o >> 1) & 3}
    a1, a2, b = ORDERS[c]
    return ((to[b] * 2 + (o & 1)) * 4 + to[a2]) * 4 + to[a1]


def sweep(src, mag, decay, masks, x, visit):
    first, last = masks
    n = len(src)
    olds = [[s(c, x, 0) for c in range(3)] for s in src]
    befores = [None] * n
    queue = []
    for y in range(MY):
        keep = [decay[c, x, y] for c in range(3)]
        stores = []
        nexts = [[src[k](c, x, y + 1) for c in range(3)] if y + 1 < MY else None for k in range(n)]
        ahead = [(src[k](1, x + 1, y), src[k](2, x + 1, y)) for k in range(n)]
        hs = [[mag[k][c, x + 1, y] for c in range(3)] for k in range(n)]
        hb = [(mag[k][1, x, y], mag[k][2, x, y]) for k in range(n)]
        for k in range(n):
            ex, ey, ez = olds[k]
            exz = jnp.where(last, 0.0, pltpu.roll(ex, MZ - 1, 1))
            eyz = jnp.where(last, 0.0, pltpu.roll(ey, MZ - 1, 1))
            eyx, ezx = ahead[k]
            h = mag[k]
            if y + 1 < MY:
                nx = nexts[k]
                gx = hs[k][0] + ((nx[2] - eyz) + (ey - ez))
                gz = hs[k][2] + ((eyx - nx[0]) + (ex - ey))
            else:
                gx = hs[k][0] + ((ey - ez) - eyz)
                gz = hs[k][2] + (eyx + (ex - ey))
            gy = hs[k][1] + ((exz - ezx) + (ez - ex))
            gxz = jnp.where(first, 0.0, pltpu.roll(gx, 1, 1))
            gyz = jnp.where(first, 0.0, pltpu.roll(gy, 1, 1))
            gyx, gzx = hb[k]
            if y > 0:
                bx, bz = befores[k]
                cx = (gz - gy) + (gyz - bz)
                cz = (gy - gx) + (bx - gyx)
            else:
                cx = (gz - gy) + gyz
                cz = (gy - gx) - gyx
            cy = (gx - gz) + (gzx - gxz)
            new = [keep[c] * olds[k][c] - 0.25 * v for c, v in enumerate((cx, cy, cz))]
            def put(k=k, y=y, old=olds[k], new=new, g=(gx, gy, gz)):
                for c in range(3):
                    mag[k][c, x + 1, y] = g[c]
                visit(k, y, old, new)
            stores.append(put)
            befores[k] = (gx, gz)
            olds[k] = nexts[k]
        queue.append(stores)
        if len(queue) > 1:
            for put in queue.pop(0):
                put()
    for stores in queue:
        for put in stores:
            put()


def kernel(ids, weight, model, source, cotangent, fields, gradient,
           wish, gather, picked, arrived, asked_v, asked_s, raw, hist, mag, decay, grad, layer, final_e,
           slots, landed, part, part_in, row_sum, row_in,
           s_raw, s_asked, s_out, s_wish, r_wish, s_a1, r_a1, s_a2, r_a2, s_b, r_b,
           s_gb, r_gb, s_g2, r_g2, s_g1, r_g1):
    me, at, core = place()
    pair = other_core(me, core, 1)
    started = []

    def go(copy):
        copy.start()
        started.append(copy)

    loads = [pltpu.make_async_copy(array, raw.at[k], s_raw.at[k]) for k, array in enumerate((source, cotangent))]
    for load in loads:
        load.start()
    barrier = pltpu.get_barrier_semaphore()
    near = neighbours(me, at, core)
    for other in near:
        pl.semaphore_signal(barrier, inc=1, device_id=(other,), device_id_type=MESH)
    for c, (a1, a2, b) in enumerate(ORDERS):
        for k in range(4):
            gather[c][0][at[a1], k] = model[pl.ds(c * 64 + k, MY, stride=4), :]
    pl.semaphore_wait(barrier, len(near))

    for k in FAR:
        for c, (a1, a2, b) in enumerate(ORDERS):
            own = gather[c][0].at[at[a1]]
            go(remote(own, own, s_a1.at[c, k], r_a1.at[c, k], shifted(me, at, a1, k)))

    def widen(j):
        for c, (a1, a2, b) in enumerate(ORDERS):
            at_j = (at[a1] + 4 - j) % 4
            slot = gather[c][0].at[at_j]
            if j:
                remote(slot, slot, s_a1.at[c, j], r_a1.at[c, j], pair).wait_recv()
            for k in FAR:
                go(remote(slot, gather[c][k].at[at_j], s_a2.at[c, k, j], r_a2.at[c, k, j], shifted(me, at, a2, k)))
    widen(0)

    lane = lax.broadcasted_iota(jnp.int32, (8, MZ), 1)

    def request(m, wanted):
        for i in range(16):
            block = ids[m, i]
            wanted = jnp.where(lane == (block >> 2), (m * 16 + i) * 4 + (block & 3), wanted)
        return wanted
    wanted = lax.fori_loop(0, 8, request, jnp.zeros((8, MZ), jnp.int32))
    wish[...] = wanted
    for c, (a1, a2, b) in enumerate(ORDERS):
        asked_v[c, 0, 0] = wanted
        for t, q in REACH:
            go(remote(wish, asked_v.at[c, t, q], s_wish.at[c, t, q], r_wish.at[c, t, q], column(me, at, core, b, t, q)))
    for j in (1, 3, 2):
        widen(j)
    for c in range(3):
        for t, q in REACH:
            remote(wish, asked_v.at[c, t, q], s_wish.at[c, t, q], r_wish.at[c, t, q], pair).wait_recv()
    loc = pltpu.make_async_copy(asked_v, asked_s, s_asked)
    loc.start()
    loc.wait()

    def place_of(b, side, row):
        return ((b * 2 + side) * 4 + row) * 4

    for k in (0, 1, 3, 2):
        for c, (a1, a2, b) in enumerate(ORDERS):
            row = (at[a2] + 4 - k) % 4
            if k:
                for j in range(4):
                    slot = gather[c][k].at[(at[a1] + 4 - j) % 4]
                    remote(slot, slot, s_a2.at[c, k, j], r_a2.at[c, k, j], pair).wait_recv()
            base = me + (row - at[a2]) * STRIDE[a2] - at[a1] * STRIDE[a1]
            spots = place_of(at[b], core, row)
            for t, q in REACH + [(0, 0)]:
                for i in range(4):
                    block = gather[c][k][i, asked_s[c, (4 - t) % 4, q, 0, base + i * STRIDE[a1]] & 3]
                    if (t, q) == (0, 0):
                        arrived[c, spots + i] = block
                    else:
                        picked[c, t, q, row, i] = block
                if (t, q) != (0, 0):
                    go(remote(picked.at[c, t, q, row], arrived.at[c, pl.ds(spots, 4)],
                              s_b.at[c, k, t, q], r_b.at[c, k, t, q], column(me, at, core, b, t, q)))

    zero = jnp.zeros((8, MZ), jnp.float32)

    def clear(i, carry):
        for c in range(3):
            for k in range(2):
                mag[k, c, i // MY, i % MY] = zero
        return carry
    lax.fori_loop(0, (MX + 1) * MY, clear, 0)

    def clear_grad(i, carry):
        for c in range(3):
            grad[c, i // MY, i % MY] = zero
        return carry
    lax.fori_loop(0, MX * MY, clear_grad, 0)

    def edge(i, carry):
        for y in range(MY):
            for k in range(2):
                for c in (1, 2):
                    hist[k, i, c, MX, y] = zero
        return carry
    lax.fori_loop(0, HALF + 1, edge, 0)
    for load in loads:
        load.wait()

    def stage(i, carry):
        for y in range(MY):
            for k in range(2):
                hist[k, 0, i // MX, i % MX, y] = raw[k, pl.ds(i * MY + y, 8, stride=3 * MX * MY), :]
        return carry
    lax.fori_loop(0, 3 * MX, stage, 0)

    for k in range(4):
        for c, (a1, a2, b) in enumerate(ORDERS):
            row = (at[a2] + 4 - k) % 4
            for t, q in REACH:
                slot = arrived.at[c, pl.ds(place_of((at[b] + 4 - t) % 4, core + (1 - 2 * core) * q, row), 4)]
                remote(slot, slot, s_b.at[c, k, t, q], r_b.at[c, k, t, q], pair).wait_recv()

    flat_decay = decay.reshape(3 * MX * MY * 8, MZ)
    flat_grad = grad.reshape(3 * MX * MY * 8, MZ)

    def blend(i, carry):
        m, x = i // MX, i % MX
        f = weight[m, x].astype(jnp.float32) * 0.125
        for c in range(3):
            close = arrived[c, spot(c, ids[m, x])]
            far = arrived[c, spot(c, ids[m, MX + x])]
            flat_decay[pl.ds((c * MX + x) * (MY * 8) + m, MY, stride=8), :] = 1.0 - 0.5 * (f * close + (1.0 - f) * far)
        return carry
    lax.fori_loop(0, 8 * MX, blend, 0)

    masks = (lane == 0, lane == MZ - 1)

    def early(n, carry):
        def plane(x, carry):
            src = [lambda c, xx, y, k=k: hist[k, n, c, xx, y] for k in range(2)]

            def visit(k, y, old, new):
                for c in range(3):
                    hist[k, n + 1, c, x, y] = new[c]
            sweep(src, [mag.at[0], mag.at[1]], decay, masks, x, visit)
            return carry
        return lax.fori_loop(0, MX, plane, carry)
    lax.fori_loop(0, HALF, early, 0)

    def late(n, carry):
        def plane(x, carry):
            src = [lambda c, xx, y, k=k: hist[k, HALF, c, xx, y] for k in range(2)]
            terms = {}

            def visit(k, y, old, new):
                terms[k] = [old[c] * hist[1 - k, STEPS - 1 - n, c, x, y] for c in range(3)]
                for c in range(3):
                    if k == 1:
                        grad[c, x, y] = grad[c, x, y] + (terms[0][c] + terms[1][c])
                    hist[k, HALF, c, x, y] = new[c]
            sweep(src, [mag.at[0], mag.at[1]], decay, masks, x, visit)
            return carry
        return lax.fori_loop(0, MX, plane, carry)
    lax.fori_loop(HALF, STEPS - 1, late, 0)

    def final(x, carry):
        src = [lambda c, xx, y: hist[0, HALF, c, xx, y]]

        def visit(k, y, old, new):
            for c in range(3):
                final_e[pl.ds((c * MX + x) * MY + y, 8, stride=3 * MX * MY), :] = new[c]
                grad[c, x, y] = grad[c, x, y] + (old[c] * hist[1, 0, c, x, y] + hist[1, HALF, c, x, y] * hist[0, 0, c, x, y])
        sweep(src, [mag.at[0]], decay, masks, x, visit)
        return carry
    lax.fori_loop(0, MX, final, 0)
    save = pltpu.make_async_copy(final_e, fields, s_out)
    save.start()

    def unstage(i, carry):
        for m in range(8):
            layer[i * 8 + m] = flat_grad[pl.ds(i * (MY * 8) + m, MY, stride=8), :]
        return carry
    lax.fori_loop(0, 3 * MX, unstage, 0)

    def landing(c, t, q, row, k, b, device):
        spots = place_of((at[b] + t) % 4, core + (1 - 2 * core) * q, row)
        return remote(slots.at[c, pl.ds(spots, 4)], landed.at[c, t, q, row], s_gb.at[c, k, t, q], r_gb.at[c, k, t, q], device)

    def rowwise(c, k, j, i, a2):
        return remote(part.at[c, k, i], part_in.at[c, k, i], s_g2.at[c, k, j], r_g2.at[c, k, j], shifted(me, at, a2, k))

    for k in (2, 1, 3, 0):
        for c, (a1, a2, b) in enumerate(ORDERS):
            row = (at[a2] + k) % 4
            for t, q in REACH + [(0, 0)]:
                side = core + (1 - 2 * core) * q
                to = (at[b] + t) % 4
                base = to * STRIDE[b] + side + row * STRIDE[a2]
                for i in range(4):
                    e = asked_s[c, 0, 0, 0, base + i * STRIDE[a1]] >> 2
                    x = e & 7
                    f = weight[e >> 4, x].astype(jnp.float32) * 0.125
                    scale = jnp.where((e & 8) == 0, f, 1.0 - f) * -0.5
                    slots[c, place_of(to, side, row) + i] = scale * layer[(c * MX + x) * 8 + (e >> 4)]
                if (t, q) != (0, 0):
                    go(landing(c, t, q, row, k, b, column(me, at, core, b, t, q)))
    for k in (2, 1, 3, 0):
        for c, (a1, a2, b) in enumerate(ORDERS):
            row = (at[a2] + k) % 4
            for t, q in REACH:
                landing(c, t, q, row, k, b, pair).wait_recv()
            base = me + (row - at[a2]) * STRIDE[a2] - at[a1] * STRIDE[a1]
            for j in (2, 1, 3, 0):
                i = (at[a1] + j) % 4
                who = asked_s[c, 0, 0, 0, base + i * STRIDE[a1]] & 3
                own = slots[c, place_of(at[b], core, row) + i]
                total = [jnp.where(who == n, own, 0.0) for n in range(4)]
                for t, q in REACH:
                    who = asked_s[c, t, q, 0, base + i * STRIDE[a1]] & 3
                    term = landed[c, t, q, row, i]
                    total = [v + jnp.where(who == n, term, 0.0) for n, v in enumerate(total)]
                for n in range(4):
                    part[c, k, i, n] = total[n]
                if k:
                    go(rowwise(c, k, j, i, a2))
    for j in (2, 1, 3, 0):
        for c, (a1, a2, b) in enumerate(ORDERS):
            i = (at[a1] + j) % 4
            for k in FAR:
                rowwise(c, k, j, i, a2).wait_recv()
            for n in range(4):
                row_sum[c, j, n] = (part[c, 0, i, n] + part_in[c, 1, i, n]) + (part_in[c, 2, i, n] + part_in[c, 3, i, n])
            if j:
                go(remote(row_sum.at[c, j], row_in.at[c, j], s_g1.at[c, j], r_g1.at[c, j], shifted(me, at, a1, j)))
    for c in range(3):
        for j in FAR:
            remote(row_sum.at[c, j], row_in.at[c, j], s_g1.at[c, j], r_g1.at[c, j], pair).wait_recv()
        for n in range(4):
            gradient[pl.ds(c * 64 + n, MY, stride=4), :] = (row_sum[c, 0, n] + row_in[c, 1, n]) + (row_in[c, 2, n] + row_in[c, 3, n])
    for copy in started:
        copy.wait_send()
    save.wait()


def run(ids, weight, model, source, cotangent):
    vmem = pl.BlockSpec(memory_space=pltpu.VMEM)
    smem = pl.BlockSpec(memory_space=pltpu.SMEM)
    anywhere = pl.BlockSpec(memory_space=pl.ANY)
    f32, i32 = jnp.float32, jnp.int32
    dma = pltpu.SemaphoreType.DMA
    rows = 8 * 3 * MX * MY
    return pl.pallas_call(
        kernel,
        out_shape=(jax.ShapeDtypeStruct((rows, MZ), f32), jax.ShapeDtypeStruct((192, MZ), f32)),
        in_specs=[smem, smem, vmem, anywhere, anywhere],
        out_specs=(anywhere, vmem),
        scratch_shapes=[
            pltpu.VMEM((8, MZ), i32),
            [[pltpu.VMEM((4, 4, MY, MZ), f32) for k in range(4)] for c in range(3)],
            pltpu.VMEM((3, 4, 2, 4, 4, MY, MZ), f32),
            pltpu.VMEM((3, 128, MY, MZ), f32),
            pltpu.VMEM((3, 4, 2, 8, MZ), i32),
            pltpu.SMEM((3, 4, 2, 8, MZ), i32),
            pltpu.VMEM((2, rows, MZ), f32),
            pltpu.VMEM((2, HALF + 1, 3, MX + 1, MY, 8, MZ), f32),
            pltpu.VMEM((2, 3, MX + 1, MY, 8, MZ), f32),
            pltpu.VMEM((3, MX, MY, 8, MZ), f32),
            pltpu.VMEM((3, MX, MY, 8, MZ), f32),
            pltpu.VMEM((3 * MX * 8, MY, MZ), f32),
            pltpu.VMEM((rows, MZ), f32),
            pltpu.VMEM((3, 128, MY, MZ), f32),
            pltpu.VMEM((3, 4, 2, 4, 4, MY, MZ), f32),
            pltpu.VMEM((3, 4, 4, 4, MY, MZ), f32),
            pltpu.VMEM((3, 4, 4, 4, MY, MZ), f32),
            pltpu.VMEM((3, 4, 4, MY, MZ), f32),
            pltpu.VMEM((3, 4, 4, MY, MZ), f32),
            dma((2,)), dma, dma,
            dma((3, 4, 2)), dma((3, 4, 2)),
            dma((3, 4)), dma((3, 4)),
            dma((3, 4, 4)), dma((3, 4, 4)),
            dma((3, 4, 4, 2)), dma((3, 4, 4, 2)),
            dma((3, 4, 4, 2)), dma((3, 4, 4, 2)),
            dma((3, 4, 4)), dma((3, 4, 4)),
            dma((3, 4)), dma((3, 4)),
        ],
        compiler_params=pltpu.CompilerParams(collective_id=0, has_side_effects=True, vmem_limit_bytes=57 * 2**20),
    )(ids, weight, model, source, cotangent)


def local(conductivity, block_ids, weights, source, cotangent):
    blocks = conductivity.shape[0]
    model = conductivity.reshape(blocks, 3, MY, MZ).transpose(1, 2, 0, 3).reshape(3 * MY * blocks, MZ)
    fields, gradient = run(block_ids, weights, model, source.reshape(-1, MZ), cotangent.reshape(-1, MZ))
    gradient = gradient.reshape(3, MY, blocks, MZ).transpose(2, 0, 1, 3)
    return fields.reshape(source.shape), gradient.reshape(conductivity.shape)


def solution(mesh):
    rows = P("dev")
    return jax.shard_map(
        local, mesh=mesh, in_specs=(rows,) * 5, out_specs=(rows, rows), check_vma=False
    )
```

time: 168 us -> 92.9 us (0.55)
  blocking collectives: 91.5 us -> 0 us
  Pallas kernels: 34.6 us -> 88.7 us
  other arithmetic: 14.1 us -> 0 us
  starting transfers between devices: 11.5 us -> 0 us
  waiting for transfers between devices: 8.15 us -> 0 us
  local copies, waits for them, and re-layouts: 7.32 us -> 3.38 us
    all_to_all x2 -> x0, blocking collectives: 91.5 us -> none  [the longest x1 45.8 us: local(): lax.all_to_all(outgoing, 'dev', split_axis=0, concat_axis=0, tiled=True)]
    pallas_call x1, Pallas kernels: 34.6 us -> 88.7 us  [run(): pl.pallas_call(kernel, out_shape=(jax.ShapeDtypeStruct((rows, MZ), f32),...]
    all_to_all x1 -> x0, starting transfers between devices: 11.5 us -> none  [local(): lax.all_to_all(wanted.reshape(count, 1), 'dev', split_axis=0, concat_axis...]
    eq x1 -> x0, other arithmetic: 11.4 us -> none  [local(): asked == k]
    all_to_all x1 -> x0, waiting for transfers between devices: 8.15 us -> none  [local(): lax.all_to_all(wanted.reshape(count, 1), 'dev', split_axis=0, concat_axis...]
    unnamed x0 -> x4, local copies, waits for them, and re-layouts: none -> 3.38 us
    all_to_all x2 -> x0, local copies, waits for them, and re-layouts: 2.71 us -> none  [the longest x1 1.96 us: local(): lax.all_to_all(outgoing, 'dev', split_axis=0, concat_axis=0, tiled=True)]
    transpose x1 -> x0, local copies, waits for them, and re-layouts: 2.09 us -> none  [local(): slots.transpose(1, 0, 2, 3)]
  transfers between devices with their start and end apart: 1 -> 0, of which waited for: 1 -> 0; matrix products, arithmetic and copies ran while one was open for 1% -> 0% of each run, Pallas kernels for 0% -> 0%
where the time goes in v2:
time: 92.9 us; the launch traced here: 92.7 us
  Pallas kernels  88.7 us (95%)
  local copies, waits for them, and re-layouts  3.38 us (4%)
    pallas_call x1, Pallas kernels, run(): pl.pallas_call(kernel, out_shape=(jax.ShapeDtypeStruct((rows, MZ), f32),...  88.7 us
    unnamed x4, local copies, waits for them, and re-layouts  3.38 us

profile of v2, /device:TPU:1, one launch (start us, length us, event | category | flops | bytes accessed | tf_op | source)
XLA Modules:
  0.0 92.7 jit_solution(275660419086538844)
XLA Ops:
  0.6 88.7 %shard_map.68 = (f32[3072,128]{1,0:T(8,128)}, f32[192,128]{1,0:T(8,128)}) custom-call(s32[8,16]{1,0:T(8,128)} %ids.1, s32[8,8]{1,0:T(8,128)} %weight.1, f32[192,128]{1,0:T(8,128)} %bitcast.16, f32[3072,128]{1,0:T(8,128)} %bitcast.13, f32[3072,128]{1,0:T(8,128)} %bitcast.14), custom_call_target="tpu_custom_call" | custom-call | tf_op jit(solution)/shard_map/pallas_call | solution.py:365
  89.3 0.0 copy-start
  89.3 2.7 %copy.11 = f32[8,3,8,16,128]{4,3,2,1,0:T(8,128)} copy(f32[8,3,8,16,128]{4,3,2,1,0:T(8,128)} %bitcast.15) | data formatting | bytes 3145728
  92.0 0.0 copy-done
  92.0 0.6 copy.12
Async XLA Ops:
  89.3 2.7 %copy-start = (f32[192,128]{1,0:T(8,128)S(1)}, f32[192,128]{1,0:T(8,128)}, u32[]{:S(2)}) copy-start(f32[192,128]{1,0:T(8,128)} %get-tuple-element.5) | copy-start | bytes 294916

commit v3 on v2

--- a/solution.py
+++ b/solution.py
@@ -54,65 +54,67 @@
     return ((to[b] * 2 + (o & 1)) * 4 + to[a2]) * 4 + to[a1]
 
 
-def sweep(src, mag, decay, masks, x, visit):
+def sweep(src, mag, decay, masks, x, visit, first_stage=True, second_stage=True):
     first, last = masks
     n = len(src)
-    olds = [[s(c, x, 0) for c in range(3)] for s in src]
+    p = x + 1
+    if first_stage:
+        olds = [[s(c, p, 0) for c in range(3)] for s in src]
     befores = [None] * n
-    queue = []
     for y in range(MY):
-        keep = [decay[c, x, y] for c in range(3)]
-        stores = []
-        nexts = [[src[k](c, x, y + 1) for c in range(3)] if y + 1 < MY else None for k in range(n)]
-        ahead = [(src[k](1, x + 1, y), src[k](2, x + 1, y)) for k in range(n)]
-        hs = [[mag[k][c, x + 1, y] for c in range(3)] for k in range(n)]
-        hb = [(mag[k][1, x, y], mag[k][2, x, y]) for k in range(n)]
-        for k in range(n):
-            ex, ey, ez = olds[k]
-            exz = jnp.where(last, 0.0, pltpu.roll(ex, MZ - 1, 1))
-            eyz = jnp.where(last, 0.0, pltpu.roll(ey, MZ - 1, 1))
-            eyx, ezx = ahead[k]
-            h = mag[k]
-            if y + 1 < MY:
-                nx = nexts[k]
-                gx = hs[k][0] + ((nx[2] - eyz) + (ey - ez))
-                gz = hs[k][2] + ((eyx - nx[0]) + (ex - ey))
-            else:
-                gx = hs[k][0] + ((ey - ez) - eyz)
-                gz = hs[k][2] + (eyx + (ex - ey))
-            gy = hs[k][1] + ((exz - ezx) + (ez - ex))
-            gxz = jnp.where(first, 0.0, pltpu.roll(gx, 1, 1))
-            gyz = jnp.where(first, 0.0, pltpu.roll(gy, 1, 1))
-            gyx, gzx = hb[k]
-            if y > 0:
-                bx, bz = befores[k]
-                cx = (gz - gy) + (gyz - bz)
-                cz = (gy - gx) + (bx - gyx)
-            else:
-                cx = (gz - gy) + gyz
-                cz = (gy - gx) - gyx
-            cy = (gx - gz) + (gzx - gxz)
-            new = [keep[c] * olds[k][c] - 0.25 * v for c, v in enumerate((cx, cy, cz))]
-            def put(k=k, y=y, old=olds[k], new=new, g=(gx, gy, gz)):
-                for c in range(3):
-                    mag[k][c, x + 1, y] = g[c]
-                visit(k, y, old, new)
-            stores.append(put)
-            befores[k] = (gx, gz)
-            olds[k] = nexts[k]
-        queue.append(stores)
-        if len(queue) > 1:
-            for put in queue.pop(0):
-                put()
-    for stores in queue:
-        for put in stores:
-            put()
+        if first_stage:
+            stores = []
+            for k in range(n):
+                ex, ey, ez = olds[k]
+                nx = [src[k](c, p, y + 1) for c in range(3)] if y + 1 < MY else None
+                eyx, ezx = src[k](1, p + 1, y), src[k](2, p + 1, y)
+                exz = jnp.where(last, 0.0, pltpu.roll(ex, MZ - 1, 1))
+                eyz = jnp.where(last, 0.0, pltpu.roll(ey, MZ - 1, 1))
+                h = mag[k]
+                if y + 1 < MY:
+                    gx = h[0, p + 1, y] + ((nx[2] - eyz) + (ey - ez))
+                    gz = h[2, p + 1, y] + ((eyx - nx[0]) + (ex - ey))
+                else:
+                    gx = h[0, p + 1, y] + ((ey - ez) - eyz)
+                    gz = h[2, p + 1, y] + (eyx + (ex - ey))
+                gy = h[1, p + 1, y] + ((exz - ezx) + (ez - ex))
+                olds[k] = nx
+                stores.append((h, gx, gy, gz))
+        if second_stage:
+            keep = [decay[c, x, y] for c in range(3)]
+            outs = []
+            for k in range(n):
+                h = mag[k]
+                gx, gy, gz = (h[c, x + 1, y] for c in range(3))
+                old = [src[k](c, x, y) for c in range(3)]
+                gxz = jnp.where(first, 0.0, pltpu.roll(gx, 1, 1))
+                gyz = jnp.where(first, 0.0, pltpu.roll(gy, 1, 1))
+                gyx, gzx = h[1, x, y], h[2, x, y]
+                if y > 0:
+                    bx, bz = befores[k]
+                    cx = (gz - gy) + (gyz - bz)
+                    cz = (gy - gx) + (bx - gyx)
+                else:
+                    cx = (gz - gy) + gyz
+                    cz = (gy - gx) - gyx
+                cy = (gx - gz) + (gzx - gxz)
+                new = [keep[c] * old[c] - 0.25 * v for c, v in enumerate((cx, cy, cz))]
+                befores[k] = (gx, gz)
+                outs.append((k, y, old, new))
+        if first_stage:
+            for h, gx, gy, gz in stores:
+                h[0, p + 1, y] = gx
+                h[1, p + 1, y] = gy
+                h[2, p + 1, y] = gz
+        if second_stage:
+            for o in outs:
+                visit(*o)
 
 
 def kernel(ids, weight, model, source, cotangent, fields, gradient,
-           wish, gather, picked, arrived, asked_v, asked_s, raw, hist, mag, decay, grad, layer, final_e,
+           wish, gather, picked, arrived, asked_v, asked_s, raw, hist, cur, mag, decay, grad, layer,
            slots, landed, part, part_in, row_sum, row_in,
-           s_raw, s_asked, s_out, s_wish, r_wish, s_a1, r_a1, s_a2, r_a2, s_b, r_b,
+           s_raw, s_asked, s_wish, r_wish, s_a1, r_a1, s_a2, r_a2, s_b, r_b,
            s_gb, r_gb, s_g2, r_g2, s_g1, r_g1):
     me, at, core = place()
     pair = other_core(me, core, 1)
@@ -209,20 +211,17 @@
         return carry
     lax.fori_loop(0, MX * MY, clear_grad, 0)
 
-    def edge(i, carry):
-        for y in range(MY):
-            for k in range(2):
-                for c in (1, 2):
-                    hist[k, i, c, MX, y] = zero
-        return carry
-    lax.fori_loop(0, HALF + 1, edge, 0)
+    for y in range(MY):
+        for k in range(2):
+            for c in (1, 2):
+                cur[k, c, MX, y] = zero
     for load in loads:
         load.wait()
 
     def stage(i, carry):
         for y in range(MY):
             for k in range(2):
-                hist[k, 0, i // MX, i % MX, y] = raw[k, pl.ds(i * MY + y, 8, stride=3 * MX * MY), :]
+                cur[k, i // MX, i % MX, y] = raw[k, pl.ds(i * MY + y, 8, stride=3 * MX * MY), :]
         return carry
     lax.fori_loop(0, 3 * MX, stage, 0)
 
@@ -248,21 +247,25 @@
 
     masks = (lane == 0, lane == MZ - 1)
 
+    state = [lambda c, x, y, k=k: cur[k, c, x, y] for k in range(2)]
+    mags = [mag.at[k] for k in range(2)]
+
     def early(n, carry):
-        def plane(x, carry):
-            src = [lambda c, xx, y, k=k: hist[k, n, c, xx, y] for k in range(2)]
-
+        def plane(x, carry, **which):
             def visit(k, y, old, new):
                 for c in range(3):
-                    hist[k, n + 1, c, x, y] = new[c]
-            sweep(src, [mag.at[0], mag.at[1]], decay, masks, x, visit)
+                    hist[k, n, c, x, y] = old[c]
+                    cur[k, c, x, y] = new[c]
+            sweep(state, mags, decay, masks, x, visit, **which)
             return carry
-        return lax.fori_loop(0, MX, plane, carry)
+        plane(-1, 0, second_stage=False)
+        lax.fori_loop(0, MX - 1, plane, carry)
+        plane(MX - 1, 0, first_stage=False)
+        return carry
     lax.fori_loop(0, HALF, early, 0)
 
     def late(n, carry):
-        def plane(x, carry):
-            src = [lambda c, xx, y, k=k: hist[k, HALF, c, xx, y] for k in range(2)]
+        def plane(x, carry, **which):
             terms = {}
 
             def visit(k, y, old, new):
@@ -270,24 +273,28 @@
                 for c in range(3):
                     if k == 1:
                         grad[c, x, y] = grad[c, x, y] + (terms[0][c] + terms[1][c])
-                    hist[k, HALF, c, x, y] = new[c]
-            sweep(src, [mag.at[0], mag.at[1]], decay, masks, x, visit)
+                    cur[k, c, x, y] = new[c]
+            sweep(state, mags, decay, masks, x, visit, **which)
             return carry
-        return lax.fori_loop(0, MX, plane, carry)
+        plane(-1, 0, second_stage=False)
+        lax.fori_loop(0, MX - 1, plane, carry)
+        plane(MX - 1, 0, first_stage=False)
+        return carry
     lax.fori_loop(HALF, STEPS - 1, late, 0)
 
-    def final(x, carry):
-        src = [lambda c, xx, y: hist[0, HALF, c, xx, y]]
-
-        def visit(k, y, old, new):
-            for c in range(3):
-                final_e[pl.ds((c * MX + x) * MY + y, 8, stride=3 * MX * MY), :] = new[c]
-                grad[c, x, y] = grad[c, x, y] + (old[c] * hist[1, 0, c, x, y] + hist[1, HALF, c, x, y] * hist[0, 0, c, x, y])
-        sweep(src, [mag.at[0]], decay, masks, x, visit)
-        return carry
-    lax.fori_loop(0, MX, final, 0)
-    save = pltpu.make_async_copy(final_e, fields, s_out)
-    save.start()
+    def final(carry):
+        def plane(x, carry, **which):
+            def visit(k, y, old, new):
+                for c in range(3):
+                    fields[pl.ds((c * MX + x) * MY + y, 8, stride=3 * MX * MY), :] = new[c]
+                    grad[c, x, y] = grad[c, x, y] + (old[c] * hist[1, 0, c, x, y] + cur[1, c, x, y] * hist[0, 0, c, x, y])
+            sweep(state[:1], mags[:1], decay, masks, x, visit, **which)
+            return carry
+        plane(-1, 0, second_stage=False)
+        lax.fori_loop(0, MX - 1, plane, carry)
+        plane(MX - 1, 0, first_stage=False)
+        return carry
+    final(0)
 
     def unstage(i, carry):
         for m in range(8):
@@ -352,7 +359,6 @@
             gradient[pl.ds(c * 64 + n, MY, stride=4), :] = (row_sum[c, 0, n] + row_in[c, 1, n]) + (row_in[c, 2, n] + row_in[c, 3, n])
     for copy in started:
         copy.wait_send()
-    save.wait()
 
 
 def run(ids, weight, model, source, cotangent):
@@ -366,7 +372,7 @@
         kernel,
         out_shape=(jax.ShapeDtypeStruct((rows, MZ), f32), jax.ShapeDtypeStruct((192, MZ), f32)),
         in_specs=[smem, smem, vmem, anywhere, anywhere],
-        out_specs=(anywhere, vmem),
+        out_specs=(vmem, vmem),
         scratch_shapes=[
             pltpu.VMEM((8, MZ), i32),
             [[pltpu.VMEM((4, 4, MY, MZ), f32) for k in range(4)] for c in range(3)],
@@ -375,19 +381,19 @@
             pltpu.VMEM((3, 4, 2, 8, MZ), i32),
             pltpu.SMEM((3, 4, 2, 8, MZ), i32),
             pltpu.VMEM((2, rows, MZ), f32),
-            pltpu.VMEM((2, HALF + 1, 3, MX + 1, MY, 8, MZ), f32),
+            pltpu.VMEM((2, HALF, 3, MX, MY, 8, MZ), f32),
+            pltpu.VMEM((2, 3, MX + 1, MY, 8, MZ), f32),
             pltpu.VMEM((2, 3, MX + 1, MY, 8, MZ), f32),
             pltpu.VMEM((3, MX, MY, 8, MZ), f32),
             pltpu.VMEM((3, MX, MY, 8, MZ), f32),
             pltpu.VMEM((3 * MX * 8, MY, MZ), f32),
-            pltpu.VMEM((rows, MZ), f32),
             pltpu.VMEM((3, 128, MY, MZ), f32),
             pltpu.VMEM((3, 4, 2, 4, 4, MY, MZ), f32),
             pltpu.VMEM((3, 4, 4, 4, MY, MZ), f32),
             pltpu.VMEM((3, 4, 4, 4, MY, MZ), f32),
             pltpu.VMEM((3, 4, 4, MY, MZ), f32),
             pltpu.VMEM((3, 4, 4, MY, MZ), f32),
-            dma((2,)), dma, dma,
+            dma((2,)), dma,
             dma((3, 4, 2)), dma((3, 4, 2)),
             dma((3, 4)), dma((3, 4)),
             dma((3, 4, 4)), dma((3, 4, 4)),
@@ -396,7 +402,7 @@
             dma((3, 4, 4)), dma((3, 4, 4)),
             dma((3, 4)), dma((3, 4)),
         ],
-        compiler_params=pltpu.CompilerParams(collective_id=0, has_side_effects=True, vmem_limit_bytes=57 * 2**20),
+        compiler_params=pltpu.CompilerParams(collective_id=0, has_side_effects=True, vmem_limit_bytes=51 * 2**20),
     )(ids, weight, model, source, cotangent)
 
 

time: 92.9 us -> 86.3 us (0.929)
  Pallas kernels: 88.7 us -> 81.4 us
    pallas_call x1, Pallas kernels: 88.7 us -> 81.4 us  [run(): pl.pallas_call(kernel, out_shape=(jax.ShapeDtypeStruct((rows, MZ), f32),...]
    unnamed x4 -> x8, local copies, waits for them, and re-layouts: 3.38 us -> 4.04 us
where the time goes in v3:
time: 86.3 us; the launch traced here: 86.1 us
  Pallas kernels  81.4 us (94%)
  local copies, waits for them, and re-layouts  4.04 us (5%)
    pallas_call x1, Pallas kernels, run(): pl.pallas_call(kernel, out_shape=(jax.ShapeDtypeStruct((rows, MZ), f32),...  81.4 us
    unnamed x8, local copies, waits for them, and re-layouts  4.04 us

profile of v3, /device:TPU:1, one launch (start us, length us, event | category | flops | bytes accessed | tf_op | source)
XLA Modules:
  0.0 86.1 jit_solution(13691043853937043681)
XLA Ops:
  0.6 0.0 copy-start
  0.6 0.9 %copy-done = f32[4,3,2048]{2,0,1:T(4,128)S(1)} copy-done((f32[4,3,2048]{2,0,1:T(4,128)S(1)}, f32[4,3,2048]{2,0,1:T(4,128)}, u32[]{:S(2)}) %copy-start) | copy-done | bytes 98328
  1.5 0.0 copy-start.1
  1.5 0.7 copy-done.1
  2.2 0.0 copy-start.2
  2.2 0.7 copy-done.2
  2.9 81.4 %shard_map.68 = (f32[3072,128]{1,0:T(8,128)S(1)}, f32[192,128]{1,0:T(8,128)S(1)}) custom-call(s32[8,16]{1,0:T(8,128)S(1)} %copy-done.1, s32[8,8]{1,0:T(8,128)S(1)} %copy-done.2, f32[192,128]{1,0:T(8,128)S(1)} %bitcast.14, f32[3072,128]{1,0:T(8,128)} %bitcast.16, f32[3072,128]{1,0:T(8,128)} %bitcast.17), custom_call_target="tpu_custom_call" | custom-call | tf_op jit(solution)/shard_map/pallas_call | solution.py:371
  84.3 1.1 %copy.11 = f32[8,3,8,16,128]{4,3,2,1,0:T(8,128)} copy(f32[8,3,8,16,128]{4,3,2,1,0:T(8,128)S(1)} %bitcast.13) | data formatting | bytes 3145728
  85.4 0.6 copy.12
Async XLA Ops:
  0.6 0.9 %copy-start = (f32[4,3,2048]{2,0,1:T(4,128)S(1)}, f32[4,3,2048]{2,0,1:T(4,128)}, u32[]{:S(2)}) copy-start(f32[4,3,2048]{2,0,1:T(4,128)} %param.5) | copy-start | bytes 294916
  1.5 0.7 copy-start.1
  2.2 0.7 copy-start.2

commit v4 on v3

--- a/solution.py
+++ b/solution.py
@@ -208,6 +208,7 @@
     def clear_grad(i, carry):
         for c in range(3):
             grad[c, i // MY, i % MY] = zero
+            decay[c, i // MY, i % MY] = zero
         return carry
     lax.fori_loop(0, MX * MY, clear_grad, 0)
 
@@ -225,28 +226,7 @@
         return carry
     lax.fori_loop(0, 3 * MX, stage, 0)
 
-    for k in range(4):
-        for c, (a1, a2, b) in enumerate(ORDERS):
-            row = (at[a2] + 4 - k) % 4
-            for t, q in REACH:
-                slot = arrived.at[c, pl.ds(place_of((at[b] + 4 - t) % 4, core + (1 - 2 * core) * q, row), 4)]
-                remote(slot, slot, s_b.at[c, k, t, q], r_b.at[c, k, t, q], pair).wait_recv()
-
-    flat_decay = decay.reshape(3 * MX * MY * 8, MZ)
-    flat_grad = grad.reshape(3 * MX * MY * 8, MZ)
-
-    def blend(i, carry):
-        m, x = i // MX, i % MX
-        f = weight[m, x].astype(jnp.float32) * 0.125
-        for c in range(3):
-            close = arrived[c, spot(c, ids[m, x])]
-            far = arrived[c, spot(c, ids[m, MX + x])]
-            flat_decay[pl.ds((c * MX + x) * (MY * 8) + m, MY, stride=8), :] = 1.0 - 0.5 * (f * close + (1.0 - f) * far)
-        return carry
-    lax.fori_loop(0, 8 * MX, blend, 0)
-
     masks = (lane == 0, lane == MZ - 1)
-
     state = [lambda c, x, y, k=k: cur[k, c, x, y] for k in range(2)]
     mags = [mag.at[k] for k in range(2)]
 
@@ -262,7 +242,37 @@
         lax.fori_loop(0, MX - 1, plane, carry)
         plane(MX - 1, 0, first_stage=False)
         return carry
-    lax.fori_loop(0, HALF, early, 0)
+
+    lax.fori_loop(0, 1, early, 0)
+
+    for k in range(4):
+        for c, (a1, a2, b) in enumerate(ORDERS):
+            row = (at[a2] + 4 - k) % 4
+            for t, q in REACH:
+                slot = arrived.at[c, pl.ds(place_of((at[b] + 4 - t) % 4, core + (1 - 2 * core) * q, row), 4)]
+                remote(slot, slot, s_b.at[c, k, t, q], r_b.at[c, k, t, q], pair).wait_recv()
+
+    flat_decay = decay.reshape(3 * MX * MY * 8, MZ)
+    flat_grad = grad.reshape(3 * MX * MY * 8, MZ)
+
+    def blend(i, carry):
+        m, x = i // MX, i % MX
+        f = weight[m, x].astype(jnp.float32) * 0.125
+        for c in range(3):
+            close = arrived[c, spot(c, ids[m, x])]
+            far = arrived[c, spot(c, ids[m, MX + x])]
+            flat_decay[pl.ds((c * MX + x) * (MY * 8) + m, MY, stride=8), :] = 1.0 - 0.5 * (f * close + (1.0 - f) * far)
+        return carry
+    lax.fori_loop(0, 8 * MX, blend, 0)
+
+    def damp(i, carry):
+        c, x = i // MX, i % MX
+        for y in range(MY):
+            for k in range(2):
+                cur[k, c, x, y] = decay[c, x, y] * hist[k, 0, c, x, y] + cur[k, c, x, y]
+        return carry
+    lax.fori_loop(0, 3 * MX, damp, 0)
+    lax.fori_loop(1, HALF, early, 0)
 
     def late(n, carry):
         def plane(x, carry, **which):
@@ -282,21 +292,10 @@
         return carry
     lax.fori_loop(HALF, STEPS - 1, late, 0)
 
-    def final(carry):
-        def plane(x, carry, **which):
-            def visit(k, y, old, new):
-                for c in range(3):
-                    fields[pl.ds((c * MX + x) * MY + y, 8, stride=3 * MX * MY), :] = new[c]
-                    grad[c, x, y] = grad[c, x, y] + (old[c] * hist[1, 0, c, x, y] + cur[1, c, x, y] * hist[0, 0, c, x, y])
-            sweep(state[:1], mags[:1], decay, masks, x, visit, **which)
-            return carry
-        plane(-1, 0, second_stage=False)
-        lax.fori_loop(0, MX - 1, plane, carry)
-        plane(MX - 1, 0, first_stage=False)
-        return carry
-    final(0)
-
     def unstage(i, carry):
+        c, x = i // MX, i % MX
+        for y in range(MY):
+            grad[c, x, y] = grad[c, x, y] + (cur[0, c, x, y] * hist[1, 0, c, x, y] + cur[1, c, x, y] * hist[0, 0, c, x, y])
         for m in range(8):
             layer[i * 8 + m] = flat_grad[pl.ds(i * (MY * 8) + m, MY, stride=8), :]
         return carry
@@ -324,6 +323,20 @@
                     slots[c, place_of(to, side, row) + i] = scale * layer[(c * MX + x) * 8 + (e >> 4)]
                 if (t, q) != (0, 0):
                     go(landing(c, t, q, row, k, b, column(me, at, core, b, t, q)))
+
+    def final(carry):
+        def plane(x, carry, **which):
+            def visit(k, y, old, new):
+                for c in range(3):
+                    fields[pl.ds((c * MX + x) * MY + y, 8, stride=3 * MX * MY), :] = new[c]
+            sweep(state[:1], mags[:1], decay, masks, x, visit, **which)
+            return carry
+        plane(-1, 0, second_stage=False)
+        lax.fori_loop(0, MX - 1, plane, carry)
+        plane(MX - 1, 0, first_stage=False)
+        return carry
+    final(0)
+
     for k in (2, 1, 3, 0):
         for c, (a1, a2, b) in enumerate(ORDERS):
             row = (at[a2] + k) % 4

time: 86.3 us -> 83.8 us (0.971)
  Pallas kernels: 81.4 us -> 78.9 us
    pallas_call x1, Pallas kernels: 81.4 us -> 78.9 us  [run(): pl.pallas_call(kernel, out_shape=(jax.ShapeDtypeStruct((rows, MZ), f32),...]
where the time goes in v4:
time: 83.8 us; the launch traced here: 83.6 us
  Pallas kernels  78.9 us (94%)
  local copies, waits for them, and re-layouts  4.04 us (5%)
    pallas_call x1, Pallas kernels, run(): pl.pallas_call(kernel, out_shape=(jax.ShapeDtypeStruct((rows, MZ), f32),...  78.9 us
    unnamed x8, local copies, waits for them, and re-layouts  4.04 us

profile of v4, /device:TPU:1, one launch (start us, length us, event | category | flops | bytes accessed | tf_op | source)
XLA Modules:
  0.0 83.6 jit_solution(4798705450999453174)
XLA Ops:
  0.6 0.0 copy-start
  0.6 0.9 %copy-done = f32[4,3,2048]{2,0,1:T(4,128)S(1)} copy-done((f32[4,3,2048]{2,0,1:T(4,128)S(1)}, f32[4,3,2048]{2,0,1:T(4,128)}, u32[]{:S(2)}) %copy-start) | copy-done | bytes 98328
  1.5 0.0 copy-start.1
  1.5 0.7 copy-done.1
  2.2 0.0 copy-start.2
  2.2 0.7 copy-done.2
  2.9 78.9 %shard_map.68 = (f32[3072,128]{1,0:T(8,128)S(1)}, f32[192,128]{1,0:T(8,128)S(1)}) custom-call(s32[8,16]{1,0:T(8,128)S(1)} %copy-done.1, s32[8,8]{1,0:T(8,128)S(1)} %copy-done.2, f32[192,128]{1,0:T(8,128)S(1)} %bitcast.14, f32[3072,128]{1,0:T(8,128)} %bitcast.16, f32[3072,128]{1,0:T(8,128)} %bitcast.17), custom_call_target="tpu_custom_call" | custom-call | tf_op jit(solution)/shard_map/pallas_call | solution.py:384
  81.8 1.1 %copy.11 = f32[8,3,8,16,128]{4,3,2,1,0:T(8,128)} copy(f32[8,3,8,16,128]{4,3,2,1,0:T(8,128)S(1)} %bitcast.13) | data formatting | bytes 3145728
  82.9 0.6 copy.12
Async XLA Ops:
  0.6 0.9 %copy-start = (f32[4,3,2048]{2,0,1:T(4,128)S(1)}, f32[4,3,2048]{2,0,1:T(4,128)}, u32[]{:S(2)}) copy-start(f32[4,3,2048]{2,0,1:T(4,128)} %param.5) | copy-start | bytes 294916
  1.5 0.7 copy-start.1
  2.2 0.7 copy-start.2

commit v5 on v4

--- a/solution.py
+++ b/solution.py
@@ -111,7 +111,7 @@
                 visit(*o)
 
 
-def kernel(ids, weight, model, source, cotangent, fields, gradient,
+def kernel(ids, model, source, cotangent, fields, gradient,
            wish, gather, picked, arrived, asked_v, asked_s, raw, hist, cur, mag, decay, grad, layer,
            slots, landed, part, part_in, row_sum, row_in,
            s_raw, s_asked, s_wish, r_wish, s_a1, r_a1, s_a2, r_a2, s_b, r_b,
@@ -257,7 +257,7 @@
 
     def blend(i, carry):
         m, x = i // MX, i % MX
-        f = weight[m, x].astype(jnp.float32) * 0.125
+        f = ids[m, 2 * MX + x].astype(jnp.float32) * 0.125
         for c in range(3):
             close = arrived[c, spot(c, ids[m, x])]
             far = arrived[c, spot(c, ids[m, MX + x])]
@@ -318,7 +318,7 @@
                 for i in range(4):
                     e = asked_s[c, 0, 0, 0, base + i * STRIDE[a1]] >> 2
                     x = e & 7
-                    f = weight[e >> 4, x].astype(jnp.float32) * 0.125
+                    f = ids[e >> 4, 2 * MX + x].astype(jnp.float32) * 0.125
                     scale = jnp.where((e & 8) == 0, f, 1.0 - f) * -0.5
                     slots[c, place_of(to, side, row) + i] = scale * layer[(c * MX + x) * 8 + (e >> 4)]
                 if (t, q) != (0, 0):
@@ -374,7 +374,7 @@
         copy.wait_send()
 
 
-def run(ids, weight, model, source, cotangent):
+def run(ids, model, source, cotangent):
     vmem = pl.BlockSpec(memory_space=pltpu.VMEM)
     smem = pl.BlockSpec(memory_space=pltpu.SMEM)
     anywhere = pl.BlockSpec(memory_space=pl.ANY)
@@ -384,7 +384,7 @@
     return pl.pallas_call(
         kernel,
         out_shape=(jax.ShapeDtypeStruct((rows, MZ), f32), jax.ShapeDtypeStruct((192, MZ), f32)),
-        in_specs=[smem, smem, vmem, anywhere, anywhere],
+        in_specs=[smem, vmem, anywhere, anywhere],
         out_specs=(vmem, vmem),
         scratch_shapes=[
             pltpu.VMEM((8, MZ), i32),
@@ -416,13 +416,13 @@
             dma((3, 4)), dma((3, 4)),
         ],
         compiler_params=pltpu.CompilerParams(collective_id=0, has_side_effects=True, vmem_limit_bytes=51 * 2**20),
-    )(ids, weight, model, source, cotangent)
+    )(ids, model, source, cotangent)
 
 
 def local(conductivity, block_ids, weights, source, cotangent):
     blocks = conductivity.shape[0]
     model = conductivity.reshape(blocks, 3, MY, MZ).transpose(1, 2, 0, 3).reshape(3 * MY * blocks, MZ)
-    fields, gradient = run(block_ids, weights, model, source.reshape(-1, MZ), cotangent.reshape(-1, MZ))
+    fields, gradient = run(jnp.concatenate([block_ids, weights], axis=1), model, source.reshape(-1, MZ), cotangent.reshape(-1, MZ))
     gradient = gradient.reshape(3, MY, blocks, MZ).transpose(2, 0, 1, 3)
     return fields.reshape(source.shape), gradient.reshape(conductivity.shape)
 

time: 83.8 us -> 83.2 us (level)
  local copies, waits for them, and re-layouts: 4.04 us -> 2.68 us
    unnamed x8 -> x4, local copies, waits for them, and re-layouts: 4.04 us -> 2.68 us
where the time goes in v5:
time: 83.2 us; the launch traced here: 83 us
  Pallas kernels  78.9 us (95%)
  local copies, waits for them, and re-layouts  2.68 us (3%)
    pallas_call x1, Pallas kernels, run(): pl.pallas_call(kernel, out_shape=(jax.ShapeDtypeStruct((rows, MZ), f32),...  78.9 us
    unnamed x4, local copies, waits for them, and re-layouts  2.68 us

profile of v5, /device:TPU:1, one launch (start us, length us, event | category | flops | bytes accessed | tf_op | source)
XLA Modules:
  0.0 83.0 jit_solution(17032363334286159995)
XLA Ops:
  0.6 0.8 pad_add_fusion.ids
  1.4 0.0 copy-start
  1.4 0.9 %copy-done = f32[4,3,2048]{2,0,1:T(4,128)S(1)} copy-done((f32[4,3,2048]{2,0,1:T(4,128)S(1)}, f32[4,3,2048]{2,0,1:T(4,128)}, u32[]{:S(2)}) %copy-start) | copy-done | bytes 98328
  2.3 78.9 %shard_map.68 = (f32[3072,128]{1,0:T(8,128)S(1)}, f32[192,128]{1,0:T(8,128)S(1)}) custom-call(s32[8,24]{1,0:T(8,128)S(1)} %pad_add_fusion.ids, f32[192,128]{1,0:T(8,128)S(1)} %bitcast.14, f32[3072,128]{1,0:T(8,128)} %bitcast.16, f32[3072,128]{1,0:T(8,128)} %bitcast.17), custom_call_target="tpu_custom_call" | custom-call | tf_op jit(solution)/shard_map/pallas_call | solution.py:384
  81.2 1.1 %copy.11 = f32[8,3,8,16,128]{4,3,2,1,0:T(8,128)} copy(f32[8,3,8,16,128]{4,3,2,1,0:T(8,128)S(1)} %bitcast.13) | data formatting | bytes 3145728
  82.4 0.6 copy.12
Async XLA Ops:
  1.4 0.9 %copy-start = (f32[4,3,2048]{2,0,1:T(4,128)S(1)}, f32[4,3,2048]{2,0,1:T(4,128)}, u32[]{:S(2)}) copy-start(f32[4,3,2048]{2,0,1:T(4,128)} %param.5) | copy-start | bytes 294916

commit v6 on v5

--- a/solution.py
+++ b/solution.py
@@ -255,15 +255,16 @@
     flat_decay = decay.reshape(3 * MX * MY * 8, MZ)
     flat_grad = grad.reshape(3 * MX * MY * 8, MZ)
 
-    def blend(i, carry):
-        m, x = i // MX, i % MX
-        f = ids[m, 2 * MX + x].astype(jnp.float32) * 0.125
-        for c in range(3):
-            close = arrived[c, spot(c, ids[m, x])]
-            far = arrived[c, spot(c, ids[m, MX + x])]
-            flat_decay[pl.ds((c * MX + x) * (MY * 8) + m, MY, stride=8), :] = 1.0 - 0.5 * (f * close + (1.0 - f) * far)
-        return carry
-    lax.fori_loop(0, 8 * MX, blend, 0)
+    def blend(m, carry):
+        for x in range(MX):
+            f = ids[m, 2 * MX + x].astype(jnp.float32) * 0.125
+            for c in range(3):
+                close = arrived[c, spot(c, ids[m, x])]
+                far = arrived[c, spot(c, ids[m, MX + x])]
+                mixed = 1.0 - 0.5 * (f * close + (1.0 - f) * far)
+                flat_decay[pl.ds((c * MX + x) * (MY * 8) + m, MY, stride=8), :] = mixed
+        return carry
+    lax.fori_loop(0, 8, blend, 0)
 
     def damp(i, carry):
         c, x = i // MX, i % MX

time: 83.2 us -> 82.2 us (0.988)
  Pallas kernels: 78.9 us -> 77.9 us
    pallas_call x1, Pallas kernels: 78.9 us -> 77.9 us  [run(): pl.pallas_call(kernel, out_shape=(jax.ShapeDtypeStruct((rows, MZ), f32),...]
where the time goes in v6:
time: 82.2 us; the launch traced here: 82 us
  Pallas kernels  77.9 us (95%)
  local copies, waits for them, and re-layouts  2.68 us (3%)
    pallas_call x1, Pallas kernels, run(): pl.pallas_call(kernel, out_shape=(jax.ShapeDtypeStruct((rows, MZ), f32),...  77.9 us
    unnamed x4, local copies, waits for them, and re-layouts  2.68 us

profile of v6, /device:TPU:1, one launch (start us, length us, event | category | flops | bytes accessed | tf_op | source)
XLA Modules:
  0.0 82.0 jit_solution(18182840539576313447)
XLA Ops:
  0.6 0.8 pad_add_fusion.ids
  1.4 0.0 copy-start
  1.4 0.9 %copy-done = f32[4,3,2048]{2,0,1:T(4,128)S(1)} copy-done((f32[4,3,2048]{2,0,1:T(4,128)S(1)}, f32[4,3,2048]{2,0,1:T(4,128)}, u32[]{:S(2)}) %copy-start) | copy-done | bytes 98328
  2.3 77.9 %shard_map.68 = (f32[3072,128]{1,0:T(8,128)S(1)}, f32[192,128]{1,0:T(8,128)S(1)}) custom-call(s32[8,24]{1,0:T(8,128)S(1)} %pad_add_fusion.ids, f32[192,128]{1,0:T(8,128)S(1)} %bitcast.14, f32[3072,128]{1,0:T(8,128)} %bitcast.16, f32[3072,128]{1,0:T(8,128)} %bitcast.17), custom_call_target="tpu_custom_call" | custom-call | tf_op jit(solution)/shard_map/pallas_call | solution.py:385
  80.2 1.1 %copy.11 = f32[8,3,8,16,128]{4,3,2,1,0:T(8,128)} copy(f32[8,3,8,16,128]{4,3,2,1,0:T(8,128)S(1)} %bitcast.13) | data formatting | bytes 3145728
  81.3 0.6 copy.12
Async XLA Ops:
  1.4 0.9 %copy-start = (f32[4,3,2048]{2,0,1:T(4,128)S(1)}, f32[4,3,2048]{2,0,1:T(4,128)}, u32[]{:S(2)}) copy-start(f32[4,3,2048]{2,0,1:T(4,128)} %param.5) | copy-start | bytes 294916
